TPU v7x, 32 devices: a whole 2x2x4 slice. The times are simulated.
32 devices in a mesh: groups: 2 (over y), row: 2 (over x), col: 4 (over z), tensor: 2 (over core).
Axes of the slice: x: 2, y: 2, z: 4, core: 2. Of those that a mesh axis runs over, the one named last changes fastest.
Arguments:
- activations: bfloat16 [2048, 14336], P(('groups', 'row', 'col'), 'tensor'), parts along dimension 0, may hold values from -320 to 320
- out_grads: bfloat16 [2048, 4096], P(('groups', 'row', 'col'), 'tensor'), parts along dimension 0, may hold values from -320 to 320
- proj_in: bfloat16 [14336, 64], P('tensor'), may hold values from -0.046875 to 0.046875
- proj_out: bfloat16 [4096, 64], P('tensor'), may hold values from -0.09375 to 0.09375
- lengths: int32 [32], P(('groups', 'row', 'col')), parts along dimension 0, may hold values from 16 to 64
- val_sketches: bfloat16 [16384, 4096], P(('groups', 'col', 'tensor'), 'row'), parts along dimension 0, may hold values from -190 to 190
Outputs:
- scores: float32 [32, 8192], P(('groups', 'row'), ('col', 'tensor')), parts along dimension 0
There are 2 independent parts, one for each index of `groups`. A program takes and returns all parts, laid end to end along the dimension named above; an argument that names none is the same for every part. Nothing has to cross between parts.
All inputs are finite; a program needn't handle non-finite values.
Results may differ from a plain program's by a relative error of at most 0.005.
Values may be sent and summed in bfloat16 or wider, within the bound.
A program may use at most 64 MiB of HBM per device.

v0:
```python
import jax
import jax.numpy as jnp
from jax import lax
from jax.sharding import PartitionSpec as P


def train_sketches(activations, out_grads, proj_in, proj_out, lengths):
    examples = lengths.shape[0]
    rank = proj_in.shape[1]
    inner = jnp.dot(activations, proj_in, preferred_element_type=jnp.float32)
    outer = jnp.dot(out_grads, proj_out, preferred_element_type=jnp.float32)
    joined = lax.psum(jnp.concatenate([inner, outer], axis=1), "tensor")
    coded = joined.astype(jnp.bfloat16).reshape(examples, -1, 2 * rank)
    slots = coded.shape[1]
    kept = (lax.broadcasted_iota(jnp.int32, (examples, slots), 1) < lengths[:, None]).astype(
        jnp.bfloat16
    )
    left = coded[:, :, :rank]
    right = coded[:, :, rank:] * kept[:, :, None]
    sketch = jnp.einsum("etk,etl->ekl", left, right, preferred_element_type=jnp.float32)
    return sketch.reshape(examples, rank * rank).astype(jnp.bfloat16)


def collect_row(pieces):
    return lax.all_gather(pieces, "col", axis=0, tiled=True)


def on_device(activations, out_grads, proj_in, proj_out, lengths, val_sketches):
    own_sketches = train_sketches(activations, out_grads, proj_in, proj_out, lengths)
    entries = own_sketches.shape[1]
    contract = (((1,), (1,)), ((), ()))
    row_sketches = collect_row(own_sketches)
    train_wide = row_sketches.astype(jnp.float32)
    train_sq = jnp.sum(train_wide * train_wide, axis=1)
    piece = lax.all_gather(val_sketches, "row", axis=1, tiled=True)
    dots = lax.dot_general(row_sketches, piece, contract, preferred_element_type=jnp.float32)
    piece_wide = piece.astype(jnp.float32)
    dots, val_sq = (dots, jnp.sum(piece_wide * piece_wide, axis=1))
    factor = jnp.sqrt(jnp.float32(entries))
    return dots * lax.rsqrt(train_sq + 1e-06)[:, None] * lax.rsqrt(val_sq + 1e-06)[None, :] * factor


def solution(mesh):
    placed = (
        P(("groups", "row", "col"), "tensor"),
        P(("groups", "row", "col"), "tensor"),
        P("tensor", None),
        P("tensor", None),
        P(("groups", "row", "col")),
        P(("groups", "col", "tensor"), "row"),
    )
    return jax.shard_map(
        on_device,
        mesh=mesh,
        in_specs=placed,
        out_specs=P(("groups", "row"), ("col", "tensor")),
        check_vma=False,
    )
```

profile of v0, /device:TPU:0, one launch (start us, length us, event | category | flops | bytes accessed | tf_op | source)
XLA Modules:
  0.0 131.3 jit_solution(6932810611739471219)
XLA Ops:
  6.5 0.0 copy-start
  6.5 0.0 all-gather.3.cloned.1.call-start
  6.5 0.7 all-gather.3.cloned.1.call-update
  7.3 1.4 %fusion.5 = f32[128,64]{0,1:T(8,128)S(1)} fusion(bf16[128,2048]{1,0:T(8,128)(2,1)} %param.7, bf16[2048,64]{0,1:T(8,128)(2,1)} %param.9), kind=kOutput, calls=%fused_computation.14 | convolution fusion | flops 33554432 | bytes 819200 | tf_op jit(solution)/shard_map/dot_general | solution.py:11
  8.7 0.0 copy-done
  8.7 1.9 %fusion.4 = f32[128,64]{0,1:T(8,128)S(1)} fusion(bf16[128,7168]{1,0:T(8,128)(2,1)S(1)} %copy-done, bf16[7168,64]{0,1:T(8,128)(2,1)} %param.8), kind=kOutput, calls=%fused_computation.13 | convolution fusion | flops 117440512 | bytes 2785280 | tf_op jit(solution)/shard_map/dot_general | solution.py:10
  10.6 3.9 %psum.7 = bf16[128,128]{0,1:T(8,128)(2,1)S(1)} all-reduce(f32[128,128]{0,1:T(8,128)S(1)} %pad_maximum_fusion), channel_id=1, replica_groups=mesh['groups'=2,'row'=2,'col'=4,'tensor'=2] {'tensor'}, use_global_device_ids=true, to_apply=%region_0.0 | all-reduce | flops 16384 | bytes 98304 | tf_op jit(solution)/shard_map/psum | solution.py:12
  14.5 0.1 copy.11
  14.7 0.7 compare_convert_fusion
  15.4 0.2 convolution_convert_fusion
  15.6 0.1 reshape.34
  15.7 14.5 %all-gather = bf16[4,2,4096]{2,1,0:T(2,128)(2,1)S(1)} all-gather(bf16[1,2,4096]{2,1,0:T(2,128)(2,1)S(1)} %reshape.34), channel_id=1, replica_groups=mesh['groups'=2,'row'=2,'col'=4,'tensor'=2] {'col'}, dimensions={0}, use_global_device_ids=true | all-gather | bytes 81920 | tf_op jit(solution)/shard_map/all_gather | solution.py:25
  30.3 0.1 multiply_reduce_fusion.1
  30.4 85.4 %all-gather.3.cloned.1.call-done = bf16[1024,4096]{1,0:T(8,128)(2,1)} async-done(((bf16[1024,2048]{1,0:T(8,128)(2,1)}), bf16[1024,4096]{1,0:T(8,128)(2,1)}) %all-gather.3.cloned.1.call-update) | async-done | bytes 8388624 | tf_op jit(solution)/shard_map/all_gather | solution.py:35
  115.8 0.0 copy-start.1
  115.8 5.2 %multiply_reduce_fusion = f32[1024]{0:T(1024)S(1)} fusion(bf16[1024,4096]{1,0:T(8,128)(2,1)} %all-gather.3.cloned.1.call-done), kind=kLoop, calls=%fused_computation | loop fusion | flops 12581888 | bytes 8392704 | tf_op jit(solution)/shard_map/reduce_sum | solution.py:38
  121.0 0.5 copy-done.1
  121.6 2.9 %fusion.1 = f32[8,1024]{1,0:T(8,128)} fusion(bf16[8,4096]{1,0:T(8,128)(2,1)S(1)} %reshape.35, bf16[1024,4096]{1,0:T(8,128)(2,1)S(1)} %copy-done.1, f32[1024]{0:T(1024)S(1)} %add_rsqrt_fusion, f32[8]{0:T(128)S(1)} %add_rsqrt_fusion.1), kind=kOutput, calls=%fused_computation.4 | convolution fusion | flops 67133440 | bytes 8491040 | tf_op jit(solution)/shard_map/dot_general | solution.py:36
  (4 shorter events, 0.1 us)
Async XLA Ops:
  6.5 2.1 %copy-start = (bf16[128,7168]{1,0:T(8,128)(2,1)S(1)}, bf16[128,7168]{1,0:T(8,128)(2,1)}, u32[]{:S(2)}) copy-start(bf16[128,7168]{1,0:T(8,128)(2,1)} %param.6) | copy-start | bytes 5505028
  6.5 109.3 %all-gather.3.cloned.1.call-start = ((), (), s32[]{:S(2)}) async-start(), calls=%async_computation | async-start | bytes 12582912 | tf_op jit(solution)/shard_map/all_gather | solution.py:35
  115.8 5.8 %copy-start.1 = (bf16[1024,4096]{1,0:T(8,128)(2,1)S(1)}, bf16[1024,4096]{1,0:T(8,128)(2,1)}, u32[]{:S(2)}) copy-start(bf16[1024,4096]{1,0:T(8,128)(2,1)} %all-gather.3.cloned.1.call-done) | copy-start | bytes 25165828
Sparse Core Ops, SparseCore 0:
  8.9 106.8 all-gather.2
where the time goes:
time: 132 us; the launch traced here: 131 us
  waiting for transfers between devices  86.1 us (65%)
  blocking collectives  18.4 us (14%)
  between operations  13.4 us (10%)
  matrix products  6.45 us (5%)
  other arithmetic  6.13 us (5%)
    all_gather x1, waiting for transfers between devices, on_device(): piece = lax.all_gather(val_sketches, 'row', axis=1, tiled=True)  85.4 us
    all_gather x1, blocking collectives, collect_row(): return lax.all_gather(pieces, 'col', axis=0, tiled=True)  14.5 us
    reduce_sum x1, other arithmetic, on_device(): dots, val_sq = (dots, jnp.sum(piece_wide * piece_wide, axis=1))  5.22 us
    psum x1, blocking collectives, train_sketches(): joined = lax.psum(jnp.concatenate([inner, outer], axis=1), 'tensor')  3.9 us
    dot_general x1, matrix products, on_device(): lax.dot_general(row_sketches, piece, contract, preferred_element_type=jnp...  2.89 us
  transfers between devices with their start and end apart: 1, of which 1 were waited for; matrix products, arithmetic and copies ran while one was open for 4% of the time, Pallas kernels for 0%

commit v1 on v0

v1 whole, which is shorter than its diff:
```python
import functools

import jax
import jax.numpy as jnp
from jax import lax
from jax.experimental import pallas as pl
from jax.experimental.pallas import tpu as pltpu
from jax.sharding import PartitionSpec as P

MESH = pl.DeviceIdType.MESH
LANES = 128
TILE = 16


def columns(start, size):
    return pl.ds(start, size)


def kernel(sizes, act_hbm, grad_hbm, win_hbm, wout_hbm, len_hbm, val_hbm, out_ref,
           act, grad, win, wout, lens, val, half, half_in, wide, packed, landed, flat, query,
           squares, vsq, vsq_in, part, part_in,
           load_sem, val_sem, pair_send, pair_recv, sk_send, sk_recv, vsq_send, vsq_recv,
           part_send, part_recv):
    R, C, T = sizes
    r, c, t = lax.axis_index("row"), lax.axis_index("col"), lax.axis_index("tensor")
    me = r * C + c
    examples = lens.shape[0]
    slots = act.shape[0] // examples
    rank = win.shape[0]
    ff = act.shape[1]
    nv, own = val.shape
    group = C * examples
    groups = own // LANES
    chunks = load_sem.shape[0] - 4
    step = ff // chunks
    vchunks = val_sem.shape[0]
    vstep = nv // vchunks

    def loops(n, body):
        if n <= 8:
            for d in range(1, n):
                body(d)
        else:
            pl.loop(1, n)(body)

    barrier = pltpu.get_barrier_semaphore()

    def greet(d):
        other = lax.rem(me + d, R * C)
        pl.semaphore_signal(barrier, inc=1, device_id={"row": other // C, "col": lax.rem(other, C)},
                            device_id_type=MESH)

    loops(R * C, greet)
    for d in range(1, T):
        pl.semaphore_signal(barrier, inc=1, device_id={"tensor": lax.rem(t + d, T)}, device_id_type=MESH)

    loads = []
    for k in range(chunks):
        cut = columns(k * step, step)
        loads.append([
            pltpu.make_async_copy(act_hbm.at[:, cut], act.at[:, cut], load_sem.at[k, 0]),
            pltpu.make_async_copy(win_hbm.at[:, cut], win.at[:, cut], load_sem.at[k, 1]),
        ])
    tail = [
        pltpu.make_async_copy(grad_hbm, grad, load_sem.at[chunks, 0]),
        pltpu.make_async_copy(wout_hbm, wout.at[0:rank], load_sem.at[chunks + 1, 0]),
        pltpu.make_async_copy(wout_hbm, wout.at[rank:2 * rank], load_sem.at[chunks + 2, 0]),
        pltpu.make_async_copy(len_hbm, lens, load_sem.at[chunks + 3, 0]),
    ]
    vloads = [
        pltpu.make_async_copy(val_hbm.at[pl.ds(k * vstep, vstep)], val.at[pl.ds(k * vstep, vstep)],
                              val_sem.at[k])
        for k in range(vchunks)
    ]
    for copy in tail:
        copy.start()
    for pair in loads:
        for copy in pair:
            copy.start()
    for copy in vloads:
        copy.start()

    contract = (((1,), (1,)), ((), ()))
    for copy in tail:
        copy.wait()
    half[rank:, :] = lax.dot_general(grad[...], wout[...], contract, preferred_element_type=jnp.float32)
    total = None
    for k in range(chunks):
        for copy in loads[k]:
            copy.wait()
        cut = slice(k * step, (k + 1) * step)
        term = lax.dot_general(win[:, cut], act[:, cut], contract, preferred_element_type=jnp.float32)
        total = term if total is None else total + term
    half[0:rank, :] = total

    pl.semaphore_wait(barrier, R * C - 1 + T - 1)

    pairs = []
    for d in range(1, T):
        other = lax.rem(t + d, T)
        copy = pltpu.make_async_remote_copy(
            half, half_in.at[t], pair_send.at[d], pair_recv.at[t],
            device_id={"tensor": other}, device_id_type=MESH)
        copy.start()
        pairs.append(copy)

    def val_squares(k):
        vloads[k].wait()
        rows = 64
        for b in range(vstep // rows):
            base = k * vstep + b * rows
            acc = None
            for g in range(groups):
                x = val[base:base + rows, g * LANES:(g + 1) * LANES].astype(jnp.float32)
                acc = x * x if acc is None else acc + x * x
            squares[base:base + rows, :] = acc

    for k in range(vchunks // 2):
        val_squares(k)

    joined = half[...]
    for d in range(1, T):
        other = lax.rem(t + d, T)
        pltpu.make_async_remote_copy(
            half, half_in.at[other], pair_send.at[d], pair_recv.at[other],
            device_id={"tensor": other}, device_id_type=MESH).wait_recv()
        joined = joined + half_in[other]
    left_t = joined[0:rank].astype(jnp.bfloat16)
    right = joined[rank:].astype(jnp.bfloat16).astype(jnp.float32)
    slot = lax.broadcasted_iota(jnp.int32, right.shape, 0)
    blocks = []
    for e in range(examples):
        kept = (slot >= e * slots) & (slot < e * slots + lens[e])
        blocks.append(jnp.where(kept, right, 0.0).astype(jnp.bfloat16))
    wide_right = jnp.concatenate(blocks, axis=1)
    outer = jnp.dot(left_t, wide_right, preferred_element_type=jnp.float32)
    lane = lax.broadcasted_iota(jnp.int32, (rank // 2, LANES), 1)
    for e in range(examples):
        wide[e] = outer[:, e * LANES:(e + 1) * LANES]
    for e in range(examples):
        even = wide[e, pl.ds(0, rank // 2, stride=2), :]
        odd = wide[e, pl.ds(1, rank // 2, stride=2), :]
        sketch = jnp.where(lane < rank, even, odd).astype(jnp.bfloat16)
        for b in range(rank // 2 // TILE):
            packed[b, e] = sketch[b * TILE:(b + 1) * TILE]

    def tile_of(row):
        return (row * groups) // TILE

    def sketch_copy(d):
        other = lax.rem(me + d, R * C)
        return pltpu.make_async_remote_copy(
            packed.at[tile_of(other // C)], landed.at[me], sk_send.at[d], sk_recv.at[me],
            device_id={"row": other // C, "col": lax.rem(other, C)}, device_id_type=MESH)

    def sketch_arrival(d):
        other = lax.rem(me + d, R * C)
        return pltpu.make_async_remote_copy(
            packed.at[0], landed.at[other], sk_send.at[d], sk_recv.at[other],
            device_id={"row": other // C, "col": lax.rem(other, C)}, device_id_type=MESH)

    loops(R * C, lambda d: sketch_copy(d).start())

    for k in range(vchunks // 2, vchunks):
        val_squares(k)
    ones = jnp.ones((8, LANES), jnp.bfloat16)
    high = squares[...].astype(jnp.bfloat16)
    low = (squares[...] - high.astype(jnp.float32)).astype(jnp.bfloat16)
    sums = (lax.dot_general(ones, high, contract, preferred_element_type=jnp.float32)
            + lax.dot_general(ones, low, contract, preferred_element_type=jnp.float32))
    vsq[...] = sums[0:1]

    def vsq_copy(d, mine):
        other = lax.rem(r + d, R)
        at = r if mine else other
        return pltpu.make_async_remote_copy(
            vsq, vsq_in.at[at], vsq_send.at[d], vsq_recv.at[at],
            device_id={"row": other}, device_id_type=MESH)

    loops(R, lambda d: vsq_copy(d, True).start())

    flat[me] = packed[tile_of(r)].astype(jnp.float32)

    def take(d):
        other = lax.rem(me + d, R * C)
        sketch_arrival(d).wait_recv()
        flat[other] = landed[other].astype(jnp.float32)

    loops(R * C, take)

    offset = lax.rem(r * groups, TILE)
    rows = flat.reshape(R * C * examples * TILE, LANES)
    train_sq = jnp.zeros((R * C * examples, LANES), jnp.float32)
    for g in range(groups):
        piece = rows[pl.ds(offset + g, R * C * examples, stride=TILE), :]
        train_sq = train_sq + piece * piece
        query[:, g * LANES:(g + 1) * LANES] = piece.astype(jnp.bfloat16)
    part[:, :, 0:LANES] = train_sq.reshape(R, group, LANES)

    def part_copy(d, k, mine):
        other = lax.rem(r + d, R)
        at = r if mine else other
        cut = columns(0, LANES + vstep) if k == 0 else columns(LANES + k * vstep, vstep)
        return pltpu.make_async_remote_copy(
            part.at[other, :, cut], part_in.at[at, :, cut], part_send.at[d, k], part_recv.at[at, k],
            device_id={"row": other}, device_id_type=MESH)

    for k in range(vchunks):
        dots = lax.dot_general(query[...], val[k * vstep:(k + 1) * vstep, :], contract,
                               preferred_element_type=jnp.float32)
        part[:, :, LANES + k * vstep:LANES + (k + 1) * vstep] = dots.reshape(R, group, vstep)
        loops(R, lambda d: part_copy(d, k, True).start())

    factor = float(rank)

    def own_sum(cut, k):
        if R <= 8:
            total = part[r, :, cut]
            for d in range(1, R):
                total = total + part_in[lax.rem(r + d, R), :, cut]
            return total
        return lax.fori_loop(1, R, lambda d, a: a + part_in[lax.rem(r + d, R), :, cut], part[r, :, cut])

    loops(R, lambda d: vsq_copy(d, False).wait_recv())
    if R <= 8:
        val_sq = vsq[...]
        for d in range(1, R):
            val_sq = val_sq + vsq_in[lax.rem(r + d, R)]
    else:
        val_sq = lax.fori_loop(1, R, lambda d, a: a + vsq_in[lax.rem(r + d, R)], vsq[...])
    val_scale = lax.rsqrt(val_sq + 1e-06)
    train_scale = None
    for k in range(vchunks):
        loops(R, lambda d: part_copy(d, k, False).wait_recv())
        if k == 0:
            train = jnp.sum(own_sum(slice(0, LANES), 0), axis=1, keepdims=True)
            train_scale = lax.rsqrt(train + 1e-06) * factor
        dots = own_sum(slice(LANES + k * vstep, LANES + (k + 1) * vstep), k)
        out_ref[:, k * vstep:(k + 1) * vstep] = (
            dots * train_scale * val_scale[:, k * vstep:(k + 1) * vstep])

    for copy in pairs:
        copy.wait_send()
    loops(R * C, lambda d: sketch_copy(d).wait_send())
    loops(R, lambda d: vsq_copy(d, True).wait_send())
    for k in range(vchunks):
        loops(R, lambda d: part_copy(d, k, True).wait_send())


def on_device(sizes, activations, out_grads, proj_in, proj_out, lengths, val_sketches):
    R, C, T = sizes
    tokens, ff = activations.shape
    width = out_grads.shape[1]
    rank = proj_in.shape[1]
    examples = lengths.shape[0]
    nv, own = val_sketches.shape
    group = C * examples
    chunks, vchunks = 4, 4
    bf16, f32 = jnp.bfloat16, jnp.float32
    tiles = rank // 2 // TILE
    scratch = [
        pltpu.VMEM((tokens, ff), bf16),
        pltpu.VMEM((tokens, width), bf16),
        pltpu.VMEM((rank, ff), bf16),
        pltpu.VMEM((2 * rank, width), bf16),
        pltpu.SMEM((examples,), jnp.int32),
        pltpu.VMEM((nv, own), bf16),
        pltpu.VMEM((rank + tokens, LANES), f32),
        pltpu.VMEM((T, rank + tokens, LANES), f32),
        pltpu.VMEM((examples, rank, LANES), f32),
        pltpu.VMEM((tiles, examples, TILE, LANES), bf16),
        pltpu.VMEM((R * C, examples, TILE, LANES), bf16),
        pltpu.VMEM((R * C, examples, TILE, LANES), f32),
        pltpu.VMEM((R * C * examples, own), bf16),
        pltpu.VMEM((nv, LANES), f32),
        pltpu.VMEM((1, nv), f32),
        pltpu.VMEM((R, 1, nv), f32),
        pltpu.VMEM((R, group, LANES + nv), f32),
        pltpu.VMEM((R, group, LANES + nv), f32),
        pltpu.SemaphoreType.DMA((chunks + 4, 2)),
        pltpu.SemaphoreType.DMA((vchunks,)),
        pltpu.SemaphoreType.DMA((T,)),
        pltpu.SemaphoreType.DMA((T,)),
        pltpu.SemaphoreType.DMA((R * C,)),
        pltpu.SemaphoreType.DMA((R * C,)),
        pltpu.SemaphoreType.DMA((R,)),
        pltpu.SemaphoreType.DMA((R,)),
        pltpu.SemaphoreType.DMA((R, vchunks)),
        pltpu.SemaphoreType.DMA((R, vchunks)),
    ]
    return pl.pallas_call(
        functools.partial(kernel, sizes),
        out_shape=jax.ShapeDtypeStruct((group, nv), f32),
        in_specs=[pl.BlockSpec(memory_space=pl.ANY)] * 6,
        out_specs=pl.BlockSpec(memory_space=pltpu.VMEM),
        scratch_shapes=scratch,
        compiler_params=pltpu.CompilerParams(
            collective_id=0, has_side_effects=True, vmem_limit_bytes=40 * 1024 * 1024
        ),
    )(activations, out_grads, proj_in.T, proj_out.T, lengths, val_sketches)


def solution(mesh):
    sizes = (mesh.shape["row"], mesh.shape["col"], mesh.shape["tensor"])
    placed = (
        P(("groups", "row", "col"), "tensor"),
        P(("groups", "row", "col"), "tensor"),
        P("tensor", None),
        P("tensor", None),
        P(("groups", "row", "col")),
        P(("groups", "col", "tensor"), "row"),
    )
    return jax.shard_map(
        functools.partial(on_device, sizes),
        mesh=mesh,
        in_specs=placed,
        out_specs=P(("groups", "row"), ("col", "tensor")),
        check_vma=False,
    )
```

time: 132 us -> 25 us (0.19)
  waiting for transfers between devices: 86.1 us -> 0 us
  blocking collectives: 18.4 us -> 0 us
  Pallas kernels: 0 us -> 16.5 us
  between operations: 13.4 us -> 0.02 us
  local copies, waits for them, and re-layouts: 0.79 us -> 8.13 us
  matrix products: 6.45 us -> 0 us
  other arithmetic: 6.13 us -> 0 us
    all_gather x1 -> x0, waiting for transfers between devices: 85.4 us -> none  [on_device(): piece = lax.all_gather(val_sketches, 'row', axis=1, tiled=True)]
    pallas_call x0 -> x1, Pallas kernels: none -> 16.5 us  [on_device(): pl.pallas_call(functools.partial(kernel, sizes), out_shape=jax.ShapeDtype...]
    all_gather x1 -> x0, blocking collectives: 14.5 us -> none  [collect_row(): return lax.all_gather(pieces, 'col', axis=0, tiled=True)]
    unnamed x6 -> x13, local copies, waits for them, and re-layouts: 0.68 us -> 8.13 us
    dot_general x4 -> x0, matrix products: 6.45 us -> none  [the longest x1 2.89 us: on_device(): lax.dot_general(row_sketches, piece, contract, preferred_element_type=jnp...]
    reduce_sum x2 -> x0, other arithmetic: 5.37 us -> none  [the longest x1 5.22 us: on_device(): dots, val_sq = (dots, jnp.sum(piece_wide * piece_wide, axis=1))]
    psum x1 -> x0, blocking collectives: 3.9 us -> none  [train_sketches(): joined = lax.psum(jnp.concatenate([inner, outer], axis=1), 'tensor')]
  transfers between devices with their start and end apart: 1 -> 0, of which waited for: 1 -> 0; matrix products, arithmetic and copies ran while one was open for 4% -> 0% of each run, Pallas kernels for 0% -> 0%
where the time goes in v1:
time: 25 us; the launch traced here: 24.6 us
  Pallas kernels  16.5 us (66%)
  local copies, waits for them, and re-layouts  8.13 us (33%)
    pallas_call x1, Pallas kernels, on_device(): pl.pallas_call(functools.partial(kernel, sizes), out_shape=jax.ShapeDtype...  16.5 us
    unnamed x13, local copies, waits for them, and re-layouts  8.13 us

profile of v1, /device:TPU:0, one launch (start us, length us, event | category | flops | bytes accessed | tf_op | source)
XLA Modules:
  0.0 24.6 jit_solution(2292148257255684191)
XLA Ops:
  0.0 0.0 copy-start
  0.0 2.2 %copy-done = bf16[1024,2048]{1,0:T(8,128)(2,1)S(1)} copy-done((bf16[1024,2048]{1,0:T(8,128)(2,1)S(1)}, bf16[1024,2048]{1,0:T(8,128)(2,1)}, u32[]{:S(2)}) %copy-start) | copy-done | bytes 4194328
  2.2 0.0 copy-start.1
  2.2 1.5 %copy-done.1 = bf16[128,7168]{1,0:T(8,128)(2,1)S(1)} copy-done((bf16[128,7168]{1,0:T(8,128)(2,1)S(1)}, bf16[128,7168]{1,0:T(8,128)(2,1)}, u32[]{:S(2)}) %copy-start.1) | copy-done | bytes 1835032
  3.7 0.0 copy-start.2
  3.7 1.2 %copy-done.2 = bf16[7168,64]{0,1:T(8,128)(2,1)S(1)} copy-done((bf16[7168,64]{0,1:T(8,128)(2,1)S(1)}, bf16[7168,64]{0,1:T(8,128)(2,1)}, u32[]{:S(2)}) %copy-start.2) | copy-done | bytes 917528
  4.9 0.0 copy-start.3
  4.9 1.0 %copy-done.3 = bf16[128,2048]{1,0:T(8,128)(2,1)S(1)} copy-done((bf16[128,2048]{1,0:T(8,128)(2,1)S(1)}, bf16[128,2048]{1,0:T(8,128)(2,1)}, u32[]{:S(2)}) %copy-start.3) | copy-done | bytes 524312
  5.9 0.0 copy-start.4
  5.9 0.9 %copy-done.4 = bf16[2048,64]{0,1:T(8,128)(2,1)S(1)} copy-done((bf16[2048,64]{0,1:T(8,128)(2,1)S(1)}, bf16[2048,64]{0,1:T(8,128)(2,1)}, u32[]{:S(2)}) %copy-start.4) | copy-done | bytes 262168
  6.9 0.0 copy-start.5
  6.9 0.7 %copy-done.5 = s32[2]{0:T(128)S(1)} copy-done((s32[2]{0:T(128)S(1)}, s32[2]{0:T(128)}, u32[]{:S(2)}) %copy-start.5) | copy-done | bytes 32
  7.5 16.5 %shard_map.64 = f32[8,1024]{1,0:T(8,128)S(1)} custom-call(bf16[128,7168]{1,0:T(8,128)(2,1)S(1)} %copy-done.1, bf16[128,2048]{1,0:T(8,128)(2,1)S(1)} %copy-done.3, bf16[64,7168]{1,0:T(8,128)(2,1)S(1)} %bitcast.2, bf16[64,2048]{1,0:T(8,128)(2,1)S(1)} %bitcast.3, s32[2]{0:T(128)S(1)} %copy-done.5, bf16[1024,2048]{1,0:T(8,128)(2,1)S(1)} %copy-done), custom_call_target="tpu_custom_call" | custom-call | tf_op jit(solution)/shard_map/pallas_call | solution.py:291
  24.0 0.6 %copy.8 = f32[8,1024]{1,0:T(8,128)} copy(f32[8,1024]{1,0:T(8,128)S(1)} %shard_map.64) | data formatting | bytes 65536
Async XLA Ops:
  0.0 2.2 %copy-start = (bf16[1024,2048]{1,0:T(8,128)(2,1)S(1)}, bf16[1024,2048]{1,0:T(8,128)(2,1)}, u32[]{:S(2)}) copy-start(bf16[1024,2048]{1,0:T(8,128)(2,1)} %val_hbm.1) | copy-start | bytes 12582916
  2.2 1.5 %copy-start.1 = (bf16[128,7168]{1,0:T(8,128)(2,1)S(1)}, bf16[128,7168]{1,0:T(8,128)(2,1)}, u32[]{:S(2)}) copy-start(bf16[128,7168]{1,0:T(8,128)(2,1)} %act_hbm.1) | copy-start | bytes 5505028
  3.7 1.2 %copy-start.2 = (bf16[7168,64]{0,1:T(8,128)(2,1)S(1)}, bf16[7168,64]{0,1:T(8,128)(2,1)}, u32[]{:S(2)}) copy-start(bf16[7168,64]{0,1:T(8,128)(2,1)} %param.8) | copy-start | bytes 2752516
  4.9 1.0 %copy-start.3 = (bf16[128,2048]{1,0:T(8,128)(2,1)S(1)}, bf16[128,2048]{1,0:T(8,128)(2,1)}, u32[]{:S(2)}) copy-start(bf16[128,2048]{1,0:T(8,128)(2,1)} %grad_hbm.1) | copy-start | bytes 1572868
  5.9 0.9 %copy-start.4 = (bf16[2048,64]{0,1:T(8,128)(2,1)S(1)}, bf16[2048,64]{0,1:T(8,128)(2,1)}, u32[]{:S(2)}) copy-start(bf16[2048,64]{0,1:T(8,128)(2,1)} %param.9) | copy-start | bytes 786436
  6.9 0.7 %copy-start.5 = (s32[2]{0:T(128)S(1)}, s32[2]{0:T(128)}, u32[]{:S(2)}) copy-start(s32[2]{0:T(128)} %len_hbm.1) | copy-start | bytes 28

commit v2 on v1

--- a/solution.py
+++ b/solution.py
@@ -291,11 +291,11 @@
     return pl.pallas_call(
         functools.partial(kernel, sizes),
         out_shape=jax.ShapeDtypeStruct((group, nv), f32),
-        in_specs=[pl.BlockSpec(memory_space=pl.ANY)] * 6,
+        in_specs=[pl.BlockSpec(memory_space=pltpu.HBM)] * 6,
         out_specs=pl.BlockSpec(memory_space=pltpu.VMEM),
         scratch_shapes=scratch,
         compiler_params=pltpu.CompilerParams(
-            collective_id=0, has_side_effects=True, vmem_limit_bytes=40 * 1024 * 1024
+            collective_id=0, has_side_effects=True, vmem_limit_bytes=56 * 1024 * 1024
         ),
     )(activations, out_grads, proj_in.T, proj_out.T, lengths, val_sketches)
 

time: 25 us -> 19.7 us (0.79)
  local copies, waits for them, and re-layouts: 8.13 us -> 1.38 us
  Pallas kernels: 16.5 us -> 18.2 us
    unnamed x13 -> x1, local copies, waits for them, and re-layouts: 8.13 us -> 1.38 us
    pallas_call x1, Pallas kernels: 16.5 us -> 18.2 us  [on_device(): pl.pallas_call(functools.partial(kernel, sizes), out_shape=jax.ShapeDtype...]
where the time goes in v2:
time: 19.7 us; the launch traced here: 19.6 us
  Pallas kernels  18.2 us (92%)
  local copies, waits for them, and re-layouts  1.38 us (7%)
    pallas_call x1, Pallas kernels, on_device(): pl.pallas_call(functools.partial(kernel, sizes), out_shape=jax.ShapeDtype...  18.2 us
    unnamed x1, local copies, waits for them, and re-layouts  1.38 us

profile of v2, /device:TPU:0, one launch (start us, length us, event | category | flops | bytes accessed | tf_op | source)
XLA Modules:
  0.0 19.6 jit_solution(6072978656694454984)
XLA Ops:
  0.0 18.2 %shard_map.64 = f32[8,1024]{1,0:T(8,128)} custom-call(bf16[128,7168]{1,0:T(8,128)(2,1)} %act_hbm.1, bf16[128,2048]{1,0:T(8,128)(2,1)} %grad_hbm.1, bf16[64,7168]{1,0:T(8,128)(2,1)} %bitcast.2, bf16[64,2048]{1,0:T(8,128)(2,1)} %bitcast.3, s32[2]{0:T(128)} %len_hbm.1, bf16[1024,2048]{1,0:T(8,128)(2,1)} %val_hbm.1), custom_call_target="tpu_custom_call" | custom-call | tf_op jit(solution)/shard_map/pallas_call | solution.py:291
  18.2 1.4 %copy.8 = f32[8,1024]{1,0:T(8,128)} copy(f32[8,1024]{1,0:T(8,128)} %shard_map.64) | data formatting | bytes 65536

commit v3 on v2

--- a/solution.py
+++ b/solution.py
@@ -255,7 +255,7 @@
     examples = lengths.shape[0]
     nv, own = val_sketches.shape
     group = C * examples
-    chunks, vchunks = 4, 4
+    chunks, vchunks = 4, 2
     bf16, f32 = jnp.bfloat16, jnp.float32
     tiles = rank // 2 // TILE
     scratch = [
@@ -295,9 +295,10 @@
         out_specs=pl.BlockSpec(memory_space=pltpu.VMEM),
         scratch_shapes=scratch,
         compiler_params=pltpu.CompilerParams(
-            collective_id=0, has_side_effects=True, vmem_limit_bytes=56 * 1024 * 1024
+            collective_id=0, has_side_effects=True, vmem_limit_bytes=32 * 1024 * 1024
         ),
-    )(activations, out_grads, proj_in.T, proj_out.T, lengths, val_sketches)
+    )(*[pltpu.with_memory_space_constraint(x, pltpu.HBM) for x in
+        (activations, out_grads, proj_in.T, proj_out.T, lengths, val_sketches)])
 
 
 def solution(mesh):

time: 19.7 us -> 17 us (0.86)
  Pallas kernels: 18.2 us -> 16.2 us
  local copies, waits for them, and re-layouts: 1.38 us -> 0.62 us
    pallas_call x1, Pallas kernels: 18.2 us -> 16.2 us  [on_device(): pl.pallas_call(functools.partial(kernel, sizes), out_shape=jax.ShapeDtype...]
    unnamed x1, local copies, waits for them, and re-layouts: 1.38 us -> 0.62 us
where the time goes in v3:
time: 17 us; the launch traced here: 16.9 us
  Pallas kernels  16.2 us (95%)
  local copies, waits for them, and re-layouts  0.62 us (4%)
    pallas_call x1, Pallas kernels, on_device(): pl.pallas_call(functools.partial(kernel, sizes), out_shape=jax.ShapeDtype...  16.2 us
    unnamed x1, local copies, waits for them, and re-layouts  0.62 us

profile of v3, /device:TPU:0, one launch (start us, length us, event | category | flops | bytes accessed | tf_op | source)
XLA Modules:
  0.0 16.9 jit_solution(9275495602077652903)
XLA Ops:
  0.0 16.2 %shard_map.64 = f32[8,1024]{1,0:T(8,128)S(1)} custom-call(bf16[128,7168]{1,0:T(8,128)(2,1)} %act_hbm.1, bf16[128,2048]{1,0:T(8,128)(2,1)} %grad_hbm.1, bf16[64,7168]{1,0:T(8,128)(2,1)} %bitcast.2, bf16[64,2048]{1,0:T(8,128)(2,1)} %bitcast.3, s32[2]{0:T(128)} %len_hbm.1, bf16[1024,2048]{1,0:T(8,128)(2,1)} %val_hbm.1), custom_call_target="tpu_custom_call" | custom-call | tf_op jit(solution)/shard_map/pallas_call | solution.py:291
  16.2 0.6 %copy.8 = f32[8,1024]{1,0:T(8,128)} copy(f32[8,1024]{1,0:T(8,128)S(1)} %shard_map.64) | data formatting | bytes 65536

commit v4 on v3

--- a/solution.py
+++ b/solution.py
@@ -77,8 +77,6 @@
     for pair in loads:
         for copy in pair:
             copy.start()
-    for copy in vloads:
-        copy.start()
 
     contract = (((1,), (1,)), ((), ()))
     for copy in tail:
@@ -88,6 +86,9 @@
     for k in range(chunks):
         for copy in loads[k]:
             copy.wait()
+        if k == chunks - 1:
+            for copy in vloads:
+                copy.start()
         cut = slice(k * step, (k + 1) * step)
         term = lax.dot_general(win[:, cut], act[:, cut], contract, preferred_element_type=jnp.float32)
         total = term if total is None else total + term
@@ -115,8 +116,6 @@
                 acc = x * x if acc is None else acc + x * x
             squares[base:base + rows, :] = acc
 
-    for k in range(vchunks // 2):
-        val_squares(k)
 
     joined = half[...]
     for d in range(1, T):
@@ -161,7 +160,7 @@
 
     loops(R * C, lambda d: sketch_copy(d).start())
 
-    for k in range(vchunks // 2, vchunks):
+    for k in range(vchunks):
         val_squares(k)
     ones = jnp.ones((8, LANES), jnp.bfloat16)
     high = squares[...].astype(jnp.bfloat16)

time: 17 us -> 16.8 us (0.988)
  Pallas kernels: 16.2 us -> 16 us
    pallas_call x1, Pallas kernels: 16.2 us -> 16 us  [on_device(): pl.pallas_call(functools.partial(kernel, sizes), out_shape=jax.ShapeDtype...]
where the time goes in v4:
time: 16.8 us; the launch traced here: 16.6 us
  Pallas kernels  16 us (95%)
  local copies, waits for them, and re-layouts  0.62 us (4%)
    pallas_call x1, Pallas kernels, on_device(): pl.pallas_call(functools.partial(kernel, sizes), out_shape=jax.ShapeDtype...  16 us
    unnamed x1, local copies, waits for them, and re-layouts  0.62 us

profile of v4, /device:TPU:0, one launch (start us, length us, event | category | flops | bytes accessed | tf_op | source)
XLA Modules:
  0.0 16.6 jit_solution(12568246712432723016)
XLA Ops:
  0.0 16.0 %shard_map.64 = f32[8,1024]{1,0:T(8,128)S(1)} custom-call(bf16[128,7168]{1,0:T(8,128)(2,1)} %act_hbm.1, bf16[128,2048]{1,0:T(8,128)(2,1)} %grad_hbm.1, bf16[64,7168]{1,0:T(8,128)(2,1)} %bitcast.2, bf16[64,2048]{1,0:T(8,128)(2,1)} %bitcast.3, s32[2]{0:T(128)} %len_hbm.1, bf16[1024,2048]{1,0:T(8,128)(2,1)} %val_hbm.1), custom_call_target="tpu_custom_call" | custom-call | tf_op jit(solution)/shard_map/pallas_call | solution.py:290
  16.0 0.6 %copy.8 = f32[8,1024]{1,0:T(8,128)} copy(f32[8,1024]{1,0:T(8,128)S(1)} %shard_map.64) | data formatting | bytes 65536

commit v5 on v4

--- a/solution.py
+++ b/solution.py
@@ -254,7 +254,7 @@
     examples = lengths.shape[0]
     nv, own = val_sketches.shape
     group = C * examples
-    chunks, vchunks = 4, 2
+    chunks, vchunks = 4, 1
     bf16, f32 = jnp.bfloat16, jnp.float32
     tiles = rank // 2 // TILE
     scratch = [

time: 16.8 us -> 16.9 us (level)
  Pallas kernels: 16 us -> 16.2 us
where the time goes in v5:
time: 16.9 us; the launch traced here: 16.8 us
  Pallas kernels  16.2 us (96%)
  local copies, waits for them, and re-layouts  0.62 us (4%)
    pallas_call x1, Pallas kernels, on_device(): pl.pallas_call(functools.partial(kernel, sizes), out_shape=jax.ShapeDtype...  16.2 us
    unnamed x1, local copies, waits for them, and re-layouts  0.62 us

profile of v5, /device:TPU:0, one launch (start us, length us, event | category | flops | bytes accessed | tf_op | source)
XLA Modules:
  0.0 16.8 jit_solution(15530882645922523954)
XLA Ops:
  0.0 16.2 %shard_map.64 = f32[8,1024]{1,0:T(8,128)S(1)} custom-call(bf16[128,7168]{1,0:T(8,128)(2,1)} %act_hbm.1, bf16[128,2048]{1,0:T(8,128)(2,1)} %grad_hbm.1, bf16[64,7168]{1,0:T(8,128)(2,1)} %bitcast.2, bf16[64,2048]{1,0:T(8,128)(2,1)} %bitcast.3, s32[2]{0:T(128)} %len_hbm.1, bf16[1024,2048]{1,0:T(8,128)(2,1)} %val_hbm.1), custom_call_target="tpu_custom_call" | custom-call | tf_op jit(solution)/shard_map/pallas_call | solution.py:290
  16.2 0.6 %copy.8 = f32[8,1024]{1,0:T(8,128)} copy(f32[8,1024]{1,0:T(8,128)S(1)} %shard_map.64) | data formatting | bytes 65536
